TPU v7x, 32 devices: a whole 2x2x4 slice. The times are simulated.
32 devices in a mesh: ctx: 8 (over z, core), comp: 4 (over y, x).
Axes of the slice: x: 2, y: 2, z: 4, core: 2. Of those that a mesh axis runs over, the one named last changes fastest.
Arguments:
- prompt_query: bfloat16 [4, 1024, 4096], P('comp', 'ctx'), may hold values from -6 to 6
- prompt_kv: bfloat16 [4, 1024, 1024], P('comp', 'ctx'), may hold values from -6 to 6
- prompt_cot: bfloat16 [4, 1024, 4096], P('comp', 'ctx'), may hold values from -6 to 6
- comp_query: bfloat16 [32, 128, 4096], P(('ctx', 'comp')), may hold values from -6 to 6
- comp_kv: bfloat16 [32, 128, 1024], P(('ctx', 'comp')), may hold values from -6 to 6
- comp_cot: bfloat16 [32, 128, 4096], P(('ctx', 'comp')), may hold values from -6 to 6
- group_of: int32 [32], replicated, may hold values from 0 to 3, as said below
- lengths: int32 [32], replicated, may hold values from 32 to 128
Outputs:
- prompt_dq: bfloat16 [4, 1024, 4096], P('comp', 'ctx')
- prompt_dkv: bfloat16 [4, 1024, 1024], P('comp', 'ctx')
- comp_dq: bfloat16 [32, 128, 4096], P(('ctx', 'comp'))
- comp_dkv: bfloat16 [32, 128, 1024], P(('ctx', 'comp'))
Inputs may be any that keep to these rules, and one draw needn't show every extreme that they name: `group_of`: each group number is named by exactly 8 completions.
All inputs are finite; a program needn't handle non-finite values.
Results may differ from a plain program's by a relative error of at most 0.023.
Values may be sent and summed in bfloat16 or wider, within the bound.
A program may use at most 128 MiB of HBM per device.

v0:
```python
import functools
import math

import jax
import jax.numpy as jnp
from jax import lax
from jax.experimental import pallas as pl
from jax.experimental.pallas import tpu as pltpu
from jax.sharding import PartitionSpec as P

QUERY_HEADS = 32
KEY_VALUE_HEADS = 4
HEAD_SIZE = 128
GROUP = QUERY_HEADS // KEY_VALUE_HEADS
HALF = KEY_VALUE_HEADS * HEAD_SIZE
PAIR = 2
SCALING = 1.0 / math.sqrt(HEAD_SIZE)

MASK_FILL = -1e30


def heads_to_rows(block, first, count):
    parts = [block[:, (first + i) * HEAD_SIZE : (first + i + 1) * HEAD_SIZE] for i in range(count)]
    return jnp.concatenate(parts, axis=0)


def head_gradients(query, cotangent, keys, values, bias, prob_ref, grad_ref, dq_ref):
    exponent = SCALING * math.log2(math.e)
    rows = query.shape[0]
    for pair in range(GROUP // PAIR):
        q = heads_to_rows(query, pair * PAIR, PAIR)
        c = heads_to_rows(cotangent, pair * PAIR, PAIR)
        scores = lax.dot_general(
            keys, q, (((1,), (1,)), ((), ())), preferred_element_type=jnp.float32
        )
        scores = bias(scores)
        prob_grad = lax.dot_general(
            values, c, (((1,), (1,)), ((), ())), preferred_element_type=jnp.float32
        )
        row_max = jnp.max(scores, axis=0, keepdims=True)
        weights = jnp.exp2((scores - row_max) * exponent)
        inverse = 1.0 / jnp.sum(weights, axis=0, keepdims=True)
        delta = jnp.sum(weights * prob_grad, axis=0, keepdims=True) * inverse
        probability = weights * inverse
        score_grad = (probability * (prob_grad - delta)).astype(jnp.bfloat16)
        columns = slice(pair * PAIR * rows, (pair + 1) * PAIR * rows)
        prob_ref[:, columns] = probability.astype(jnp.bfloat16)
        grad_ref[:, columns] = score_grad
        dq = lax.dot_general(
            score_grad, keys, (((0,), (0,)), ((), ())), preferred_element_type=jnp.float32
        )
        dq = (dq * SCALING).astype(jnp.bfloat16)
        for i in range(PAIR):
            at = (pair * PAIR + i) * HEAD_SIZE
            dq_ref[:, at : at + HEAD_SIZE] = dq[i * rows : (i + 1) * rows]
    key_grad = jnp.dot(
        grad_ref[...], heads_to_rows(query, 0, GROUP), preferred_element_type=jnp.float32
    )
    value_grad = jnp.dot(
        prob_ref[...], heads_to_rows(cotangent, 0, GROUP), preferred_element_type=jnp.float32
    )
    return (key_grad * SCALING).astype(jnp.bfloat16), value_grad.astype(jnp.bfloat16)


def prompt_kernel(place_ref, q_ref, c_ref, k_ref, v_ref, dq_ref, dk_ref, dv_ref, bias_ref, prob_ref, grad_ref):
    rows = q_ref.shape[0]
    total = k_ref.shape[0]

    @pl.when(pl.program_id(0) == 0)
    def _():
        shape = (total, rows)
        key_at = lax.broadcasted_iota(jnp.int32, shape, 0)
        row_at = lax.broadcasted_iota(jnp.int32, shape, 1)
        allowed = key_at <= row_at + place_ref[0] * rows
        bias_ref[...] = jnp.where(allowed, 0.0, MASK_FILL)

    def bias(scores):
        return scores + jnp.concatenate([bias_ref[...]] * PAIR, axis=1)

    dk, dv = head_gradients(
        q_ref[...], c_ref[...], k_ref[...], v_ref[...], bias, prob_ref, grad_ref, dq_ref
    )
    dk_ref[...] = dk
    dv_ref[...] = dv


def completion_kernel(length_ref, q_ref, c_ref, k_ref, v_ref, own_k_ref, own_v_ref, dq_ref, dk_ref, dv_ref, own_dk_ref, own_dv_ref, prob_ref, grad_ref):
    rows = q_ref.shape[0]
    total = k_ref.shape[0]
    length = length_ref[0]
    key_at = lax.broadcasted_iota(jnp.int32, (rows, rows), 0)
    row_at = lax.broadcasted_iota(jnp.int32, (rows, rows), 1)
    own_bias = jnp.where((key_at <= row_at) & (key_at < length), 0.0, MASK_FILL)

    def bias(scores):
        own = scores[total:] + jnp.concatenate([own_bias] * PAIR, axis=1)
        return jnp.concatenate([scores[:total], own], axis=0)

    cotangent = c_ref[...]
    live = lax.broadcasted_iota(jnp.int32, cotangent.shape, 0) < length
    cotangent = jnp.where(live, cotangent, jnp.zeros_like(cotangent))
    keys = jnp.concatenate([k_ref[...], own_k_ref[...]], axis=0)
    values = jnp.concatenate([v_ref[...], own_v_ref[...]], axis=0)
    dk, dv = head_gradients(q_ref[...], cotangent, keys, values, bias, prob_ref, grad_ref, dq_ref)
    dk_ref[...] = dk[:total]
    dv_ref[...] = dv[:total]
    own_dk_ref[...] = dk[total:]
    own_dv_ref[...] = dv[total:]


def lane_block(rows, width, shift=0):
    return pl.BlockSpec((rows, width), lambda h, _: (0, h + shift))


def params():
    return pltpu.CompilerParams(vmem_limit_bytes=56 * 1024 * 1024)


def prompt_attention(query, cotangent, kv, place):
    rows, total = query.shape[0], kv.shape[0]
    wide = GROUP * HEAD_SIZE
    return pl.pallas_call(
        prompt_kernel,
        grid_spec=pltpu.PrefetchScalarGridSpec(
            num_scalar_prefetch=1,
            grid=(KEY_VALUE_HEADS,),
            in_specs=[
                lane_block(rows, wide),
                lane_block(rows, wide),
                lane_block(total, HEAD_SIZE),
                lane_block(total, HEAD_SIZE, KEY_VALUE_HEADS),
            ],
            out_specs=[
                lane_block(rows, wide),
                lane_block(total, HEAD_SIZE),
                lane_block(total, HEAD_SIZE),
            ],
            scratch_shapes=[
                pltpu.VMEM((total, rows), jnp.float32),
                pltpu.VMEM((total, GROUP * rows), jnp.bfloat16),
                pltpu.VMEM((total, GROUP * rows), jnp.bfloat16),
            ],
        ),
        out_shape=[
            jax.ShapeDtypeStruct(query.shape, jnp.bfloat16),
            jax.ShapeDtypeStruct((total, HALF), jnp.bfloat16),
            jax.ShapeDtypeStruct((total, HALF), jnp.bfloat16),
        ],
        compiler_params=params(),
        name="prompt_attention",
    )(place, query, cotangent, kv, kv)


def completion_attention(query, cotangent, kv, own_kv, length):
    rows, total = query.shape[0], kv.shape[0]
    wide = GROUP * HEAD_SIZE
    return pl.pallas_call(
        completion_kernel,
        grid_spec=pltpu.PrefetchScalarGridSpec(
            num_scalar_prefetch=1,
            grid=(KEY_VALUE_HEADS,),
            in_specs=[
                lane_block(rows, wide),
                lane_block(rows, wide),
                lane_block(total, HEAD_SIZE),
                lane_block(total, HEAD_SIZE, KEY_VALUE_HEADS),
                lane_block(rows, HEAD_SIZE),
                lane_block(rows, HEAD_SIZE, KEY_VALUE_HEADS),
            ],
            out_specs=[
                lane_block(rows, wide),
                lane_block(total, HEAD_SIZE),
                lane_block(total, HEAD_SIZE),
                lane_block(rows, HEAD_SIZE),
                lane_block(rows, HEAD_SIZE),
            ],
            scratch_shapes=[
                pltpu.VMEM((total + rows, GROUP * rows), jnp.bfloat16),
                pltpu.VMEM((total + rows, GROUP * rows), jnp.bfloat16),
            ],
        ),
        out_shape=[
            jax.ShapeDtypeStruct(query.shape, jnp.bfloat16),
            jax.ShapeDtypeStruct((total, HALF), jnp.bfloat16),
            jax.ShapeDtypeStruct((total, HALF), jnp.bfloat16),
            jax.ShapeDtypeStruct((rows, HALF), jnp.bfloat16),
            jax.ShapeDtypeStruct((rows, HALF), jnp.bfloat16),
        ],
        compiler_params=params(),
        name="completion_attention",
    )(length, query, cotangent, kv, kv, own_kv, own_kv)


def local(prompt_query, prompt_kv, prompt_cot, comp_query, comp_kv, comp_cot, group_of, lengths):
    ctx_count = lax.axis_size("ctx")
    comp_count = lax.axis_size("comp")
    ctx_place = lax.axis_index("ctx")
    comp_place = lax.axis_index("comp")
    prompt_rows = prompt_query.shape[1]
    whole_prompt = lax.all_gather(prompt_kv[0], "ctx", axis=0, tiled=True)
    column_groups = jnp.take(group_of.reshape(ctx_count, comp_count), comp_place, axis=1)
    stacked_blocks = lax.all_gather(prompt_kv, "comp", axis=0, tiled=True)
    outgoing = jnp.take(stacked_blocks, column_groups, axis=0)
    incoming = lax.all_to_all(outgoing, "ctx", split_axis=0, concat_axis=0, tiled=True)
    group_prompt = incoming.reshape(-1, incoming.shape[2])
    length = lax.dynamic_slice_in_dim(lengths, ctx_place * comp_count + comp_place, 1)
    comp_dq, comp_dk, comp_dv, own_dk, own_dv = completion_attention(
        comp_query[0], comp_cot[0], group_prompt, comp_kv[0], length
    )
    prompt_dq, prompt_dk, prompt_dv = prompt_attention(
        prompt_query[0], prompt_cot[0], whole_prompt, ctx_place.reshape(1)
    )
    comp_terms = jnp.concatenate([comp_dk, comp_dv], axis=1)
    prompt_terms = jnp.concatenate([prompt_dk, prompt_dv], axis=1)
    outgoing_terms = comp_terms.reshape(ctx_count, prompt_rows, 2 * HALF)
    returned = lax.all_to_all(outgoing_terms, "ctx", split_axis=0, concat_axis=0, tiled=True)
    chooser = column_groups[:, None] == jnp.arange(comp_count, dtype=jnp.int32)[None, :]
    group_table = jnp.einsum(
        "sg,srw->grw",
        chooser.astype(jnp.bfloat16),
        returned,
        preferred_element_type=jnp.float32,
    )
    own_terms = lax.psum_scatter(prompt_terms, "ctx", scatter_dimension=0, tiled=True)
    group_sum = lax.psum_scatter(
        group_table.astype(jnp.bfloat16), "comp", scatter_dimension=0, tiled=True
    )[0]
    summed = group_sum.astype(jnp.float32) + own_terms.astype(jnp.float32)
    return (
        prompt_dq[None],
        summed.astype(jnp.bfloat16)[None],
        comp_dq[None],
        jnp.concatenate([own_dk, own_dv], axis=1)[None],
    )


def solution(mesh):
    placed = (
        P("comp", "ctx", None),
        P("comp", "ctx", None),
        P("comp", "ctx", None),
        P(("ctx", "comp"), None, None),
        P(("ctx", "comp"), None, None),
        P(("ctx", "comp"), None, None),
        P(),
        P(),
    )
    return jax.shard_map(
        local,
        mesh=mesh,
        in_specs=placed,
        out_specs=(
            P("comp", "ctx", None),
            P("comp", "ctx", None),
            P(("ctx", "comp"), None, None),
            P(("ctx", "comp"), None, None),
        ),
        check_vma=False,
    )
```

profile of v0, /device:TPU:9, one launch (start us, length us, event | category | flops | bytes accessed | tf_op | source)
XLA Modules:
  0.0 234.4 jit_solution(7217230146459832753)
XLA Ops:
  7.2 0.0 all-gather.4.cloned.1.call-start
  7.2 0.7 all-gather.4.cloned.1.call-update
  7.9 0.0 all-gather.6.cloned.1.call-start
  7.9 0.7 all-gather.6.cloned.1.call-update
  8.7 0.7 reshape.50
  9.4 0.2 fusion.8
  9.6 28.1 %all-gather.4.cloned.1.call-done = bf16[4,128,1024]{2,1,0:T(8,128)(2,1)} async-done(((bf16[1,128,1024]{2,1,0:T(8,128)(2,1)}), bf16[4,128,1024]{2,1,0:T(8,128)(2,1)}) %all-gather.4.cloned.1.call-update) | async-done | bytes 1048592 | tf_op jit(solution)/shard_map/all_gather | solution.py:202
  37.7 1.9 gather_fusion
  39.6 1.6 broadcast_select_fusion
  41.2 5.5 %all-to-all-start = ((bf16[8,128,1024]{2,1,0:T(8,128)(2,1)}), bf16[8,128,1024]{2,1,0:T(8,128)(2,1)S(1)}, u32[]{:S(2)}, u32[]{:S(2)}) async-start(bf16[8,128,1024]{2,1,0:T(8,128)(2,1)} %broadcast_select_fusion), calls=%async_computation | async-start | bytes 4194304 | tf_op jit(solution)/shard_map/all_to_all | solution.py:204
  46.6 0.0 reduce-scatter.5.cloned.1.call-start
  46.6 39.0 %all-gather.6.cloned.1.call-done = bf16[1,1024,1024]{2,1,0:T(8,128)(2,1)} async-done(((bf16[1,128,1024]{2,1,0:T(8,128)(2,1)}), bf16[1,1024,1024]{2,1,0:T(8,128)(2,1)}) %all-gather.6.cloned.1.call-update) | async-done | bytes 2097168 | tf_op jit(solution)/shard_map/all_gather | solution.py:200
  85.6 22.4 %prompt_attention.1 = (bf16[128,4096]{1,0:T(8,128)(2,1)}, bf16[1024,512]{1,0:T(8,128)(2,1)}, bf16[1024,512]{1,0:T(8,128)(2,1)}) custom-call(s32[1]{0:T(128)} %bitcast.place_ref, bf16[128,4096]{1,0:T(8,128)(2,1)} %bitcast.27, bf16[128,4096]{1,0:T(8,128)(2,1)} %bitcast.28, bf16[1024,1024]{1,0:T(8,128)(2,1)} %bitcast.24, bf16[1024,1024]{1,0:T(8,128)(2,1)} %bitcast.25), custom_call_target="tpu_custom_call" | custom-call | tf_op jit(solution)/shard_map/prompt_attention/pallas_call | solution.py:122
  108.1 3.1 %pad_maximum_fusion.1 = bf16[1024,1024]{1,0:T(8,128)(2,1)} fusion(bf16[1024,512]{1,0:T(8,128)(2,1)} %get-tuple-element.16, bf16[1024,512]{1,0:T(8,128)(2,1)} %get-tuple-element.15), kind=kLoop, calls=%fused_computation.2 | loop fusion | flops 4194304 | bytes 4194304 | tf_op jit(solution)/shard_map/concatenate | solution.py:214
  111.2 0.0 copy-start.3
  111.2 0.0 reduce-scatter.5.cloned.1.call-update
  111.2 0.0 reduce-scatter.7.cloned.1.call-start
  111.3 0.6 copy-done.3
  111.9 0.6 dynamic_slice.3.length_ref
  112.5 0.0 all-to-all-done
  112.5 0.0 copy-start
  112.5 1.3 copy-done
  113.8 24.4 %completion_attention.1 = (bf16[128,4096]{1,0:T(8,128)(2,1)}, bf16[1024,512]{1,0:T(8,128)(2,1)}, bf16[1024,512]{1,0:T(8,128)(2,1)}, bf16[128,512]{1,0:T(8,128)(2,1)}, bf16[128,512]{1,0:T(8,128)(2,1)}) custom-call(s32[1]{0:T(128)} %dynamic_slice.3.length_ref, bf16[128,4096]{1,0:T(8,128)(2,1)} %bitcast.31, bf16[128,4096]{1,0:T(8,128)(2,1)} %bitcast.32, ...), custom_call_target="tpu_custom_call" | custom-call | tf_op jit(solution)/shard_map/completion_attention/pallas_call | solution.py:157
  138.2 1.8 pad_maximum_fusion
  140.0 54.8 %all_to_all.10 = bf16[8,128,1024]{2,1,0:T(8,128)(2,1)S(1)} all-to-all(bf16[8,128,1024]{2,1,0:T(8,128)(2,1)S(1)} %bitcast.26), channel_id=1, replica_groups=mesh['ctx'=8,'comp'=4] {'ctx'}, dimensions={0} | all-to-all | bytes 4194304 | tf_op jit(solution)/shard_map/all_to_all | solution.py:216
  194.8 1.4 fusion.2
  196.2 0.0 copy-start.1
  196.2 0.0 copy-start.2
  196.2 1.3 copy.17
  197.5 0.0 reduce-scatter.7.cloned.1.call-update
  197.5 0.0 copy-done.1
  197.5 0.0 copy-done.2
  197.6 0.7 maximum_bitcast_fusion
  198.3 0.0 reduce-scatter.5.cloned.1.call-done
  198.3 27.8 %reduce-scatter.7.cloned.1.call-done = bf16[1,128,1024]{2,1,0:T(8,128)(2,1)} async-done(((bf16[4,128,1024]{2,1,0:T(8,128)(2,1)}), bf16[1,128,1024]{2,1,0:T(8,128)(2,1)}) %reduce-scatter.7.cloned.1.call-update) | async-done | bytes 262160
  226.1 1.8 fusion.6
  (2 shorter events, 0.0 us)
Async XLA Ops:
  7.2 30.5 %all-gather.4.cloned.1.call-start = ((), (), s32[]{:S(2)}) async-start(), calls=%async_computation.4 | async-start | bytes 1310720 | tf_op jit(solution)/shard_map/all_gather | solution.py:202
  7.9 77.7 %all-gather.6.cloned.1.call-start = ((), (), s32[]{:S(2)}) async-start(), calls=%async_computation.6 | async-start | bytes 2359296 | tf_op jit(solution)/shard_map/all_gather | solution.py:200
  41.2 71.3 %all-to-all-start = ((bf16[8,128,1024]{2,1,0:T(8,128)(2,1)}), bf16[8,128,1024]{2,1,0:T(8,128)(2,1)S(1)}, u32[]{:S(2)}, u32[]{:S(2)}) async-start(bf16[8,128,1024]{2,1,0:T(8,128)(2,1)} %broadcast_select_fusion), calls=%async_computation | async-start | bytes 4194304 | tf_op jit(solution)/shard_map/all_to_all | solution.py:204
  46.6 151.7 %reduce-scatter.5.cloned.1.call-start = ((), (), s32[]{:S(2)}) async-start(), calls=%async_computation.5 | async-start | bytes 2359296 | tf_op jit(solution)/shard_map/reduce_scatter | solution.py:224
  111.2 0.7 copy-start.3
  111.2 114.8 %reduce-scatter.7.cloned.1.call-start = ((), (), s32[]{:S(2)}) async-start(), calls=%async_computation.7 | async-start | bytes 1310720
  112.5 1.3 copy-start
  196.2 1.3 copy-start.1
  196.2 1.3 copy-start.2
Sparse Core Ops, SparseCore 0:
  9.8 27.7 all-gather.3
  39.3 46.2 all-gather.5
  111.3 34.3 reduce-scatter.4
  197.7 28.3 reduce-scatter.6
where the time goes:
time: 236 us; the launch traced here: 234 us
  waiting for transfers between devices  96.2 us (41%)
  blocking collectives  54.8 us (23%)
  Pallas kernels  46.8 us (20%)
  between operations  13.8 us (6%)
  other arithmetic  9.27 us (4%)
  local copies, waits for them, and re-layouts  6.46 us (3%)
  starting transfers between devices  5.58 us (2%)
    all_to_all x1, blocking collectives, local(): lax.all_to_all(outgoing_terms, 'ctx', split_axis=0, concat_axis=0, tiled=...  54.8 us
    all_gather x1, waiting for transfers between devices, local(): whole_prompt = lax.all_gather(prompt_kv[0], 'ctx', axis=0, tiled=True)  39 us
    unnamed x5, waiting for transfers between devices  29.2 us
    all_gather x1, waiting for transfers between devices, local(): stacked_blocks = lax.all_gather(prompt_kv, 'comp', axis=0, tiled=True)  28.1 us
    pallas_call x1, Pallas kernels, completion_attention(): pl.pallas_call(completion_kernel, grid_spec=pltpu.PrefetchScalarGridSpec(...  24.4 us
    pallas_call x1, Pallas kernels, prompt_attention(): pl.pallas_call(prompt_kernel, grid_spec=pltpu.PrefetchScalarGridSpec(num_...  22.4 us
    all_to_all x1, starting transfers between devices, local(): lax.all_to_all(outgoing, 'ctx', split_axis=0, concat_axis=0, tiled=True)  5.46 us
  transfers between devices with their start and end apart: 5, of which 3 were waited for; matrix products, arithmetic and copies ran while one was open for 6% of the time, Pallas kernels for 20%

commit v1 on v0

v1 whole, which is shorter than its diff:
```python
import functools
import math

import jax
import jax.numpy as jnp
from jax import lax
from jax.experimental import pallas as pl
from jax.experimental.pallas import tpu as pltpu
from jax.sharding import PartitionSpec as P

QUERY_HEADS = 32
KEY_VALUE_HEADS = 4
HEAD_SIZE = 128
GROUP = QUERY_HEADS // KEY_VALUE_HEADS
HALF = KEY_VALUE_HEADS * HEAD_SIZE
PAIR = 2
SCALING = 1.0 / math.sqrt(HEAD_SIZE)

MASK_FILL = -1e30


def heads_to_rows(block, first, count):
    parts = [block[:, (first + i) * HEAD_SIZE : (first + i + 1) * HEAD_SIZE] for i in range(count)]
    return jnp.concatenate(parts, axis=0)


def head_gradients(query, cotangent, keys, values, bias, prob_ref, grad_ref, dq_ref):
    exponent = SCALING * math.log2(math.e)
    rows = query.shape[0]
    for pair in range(GROUP // PAIR):
        q = heads_to_rows(query, pair * PAIR, PAIR)
        c = heads_to_rows(cotangent, pair * PAIR, PAIR)
        scores = lax.dot_general(
            keys, q, (((1,), (1,)), ((), ())), preferred_element_type=jnp.float32
        )
        scores = bias(scores)
        prob_grad = lax.dot_general(
            values, c, (((1,), (1,)), ((), ())), preferred_element_type=jnp.float32
        )
        row_max = jnp.max(scores, axis=0, keepdims=True)
        weights = jnp.exp2((scores - row_max) * exponent)
        inverse = 1.0 / jnp.sum(weights, axis=0, keepdims=True)
        delta = jnp.sum(weights * prob_grad, axis=0, keepdims=True) * inverse
        probability = weights * inverse
        score_grad = (probability * (prob_grad - delta)).astype(jnp.bfloat16)
        columns = slice(pair * PAIR * rows, (pair + 1) * PAIR * rows)
        prob_ref[:, columns] = probability.astype(jnp.bfloat16)
        grad_ref[:, columns] = score_grad
        dq = lax.dot_general(
            score_grad, keys, (((0,), (0,)), ((), ())), preferred_element_type=jnp.float32
        )
        dq = (dq * SCALING).astype(jnp.bfloat16)
        for i in range(PAIR):
            at = (pair * PAIR + i) * HEAD_SIZE
            dq_ref[:, at : at + HEAD_SIZE] = dq[i * rows : (i + 1) * rows]
    key_grad = jnp.dot(
        grad_ref[...], heads_to_rows(query, 0, GROUP), preferred_element_type=jnp.float32
    )
    value_grad = jnp.dot(
        prob_ref[...], heads_to_rows(cotangent, 0, GROUP), preferred_element_type=jnp.float32
    )
    return (key_grad * SCALING).astype(jnp.bfloat16), value_grad.astype(jnp.bfloat16)


def remote(source, target, send, receive, ctx, comp):
    return pltpu.make_async_remote_copy(
        src_ref=source,
        dst_ref=target,
        send_sem=send,
        recv_sem=receive,
        device_id=(ctx, comp),
        device_id_type=pl.DeviceIdType.MESH,
    )


def greet(devices):
    barrier = pltpu.get_barrier_semaphore()
    for device in devices:
        pl.semaphore_signal(
            barrier, inc=1, device_id=device, device_id_type=pl.DeviceIdType.MESH
        )
    pl.semaphore_wait(barrier, len(devices))


def prompt_kernel(
    ctx_count, comp_count, q_ref, c_ref, kv_ref, dq_ref, dk_ref, dv_ref, all_ref,
    whole, bias_ref, prob_ref, grad_ref,
    up_send, up_recv, down_send, down_recv, pair_send, pair_recv,
    side_send, side_recv, pass_send, pass_recv, keep_sem,
):
    step = pl.program_id(0)
    place = lax.axis_index("ctx")
    column = lax.axis_index("comp")
    rows = q_ref.shape[0]
    total = ctx_count * rows
    chips = ctx_count // 2
    chip, core = place // 2, place % 2
    sibling = chip * 2 + 1 - core

    def other(offset):
        return (column + offset) % comp_count

    def up(t):
        at = (chip - t) * 2 + core
        return remote(whole.at[at], whole.at[at], up_send.at[t], up_recv.at[t], place + 2, column)

    def up_arrival(t):
        at = (chip - 1 - t) * 2 + core
        return remote(whole.at[at], whole.at[at], up_send.at[t], up_recv.at[t], place - 2, column)

    def down(t):
        at = (chip + t) * 2 + core
        return remote(
            whole.at[at], whole.at[at], down_send.at[t], down_recv.at[t], place - 2, column
        )

    def down_arrival(t):
        at = (chip + 1 + t) * 2 + core
        return remote(
            whole.at[at], whole.at[at], down_send.at[t], down_recv.at[t], place + 2, column
        )

    def to_sibling(k, side):
        at = k * 2 + side
        return remote(
            whole.at[at], whole.at[at], pair_send.at[k], pair_recv.at[k], sibling, column
        )

    def to_column(k, e):
        at = k * 2 + core
        return remote(
            whole.at[at],
            all_ref.at[column, at],
            side_send.at[e - 1, k],
            side_recv.at[e - 1, k],
            place,
            other(e),
        )

    def from_column(k, e):
        at = k * 2 + core
        source = other(comp_count - e)
        return remote(
            whole.at[at],
            all_ref.at[source, at],
            side_send.at[e - 1, k],
            side_recv.at[e - 1, k],
            place,
            source,
        )

    def pass_on(k, e, side):
        at = k * 2 + side
        source = other(comp_count - e)
        return remote(
            all_ref.at[source, at],
            all_ref.at[source, at],
            pass_send.at[e - 1, k],
            pass_recv.at[e - 1, k],
            sibling,
            column,
        )

    keep = pltpu.make_async_copy(whole, all_ref.at[column], keep_sem)

    def share(k):
        to_sibling(k, core).start()
        for e in range(1, comp_count):
            to_column(k, e).start()

    @pl.when(step == 0)
    def _():
        whole[place] = kv_ref[...]
        greetings = [(sibling, column)]
        greetings += [(place, other(e)) for e in range(1, comp_count)]
        greet(greetings + [
            ((place + 2) % ctx_count, column),
            ((place + ctx_count - 2) % ctx_count, column),
        ])
        for t in range(chips - 1):

            @pl.when((chip - t >= 0) & (chip + 1 < chips))
            def _():
                up(t).start()

            @pl.when((chip + t < chips) & (chip >= 1))
            def _():
                down(t).start()

            if t == 0:
                share(chip)

            @pl.when(chip - 1 - t >= 0)
            def _():
                up_arrival(t).wait_recv()
                share(chip - 1 - t)

            @pl.when(chip + 1 + t < chips)
            def _():
                down_arrival(t).wait_recv()
                share(chip + 1 + t)

        for k in range(chips):
            to_sibling(k, 1 - core).wait_recv()
        keep.start()
        shape = (total, rows)
        key_at = lax.broadcasted_iota(jnp.int32, shape, 0)
        row_at = lax.broadcasted_iota(jnp.int32, shape, 1)
        bias_ref[...] = jnp.where(key_at <= row_at + place * rows, 0.0, MASK_FILL)

    def bias(scores):
        return scores + jnp.concatenate([bias_ref[...]] * PAIR, axis=1)

    def head_of(shift):
        at = pl.multiple_of((step + shift) * HEAD_SIZE, HEAD_SIZE)
        return whole[:, :, pl.ds(at, HEAD_SIZE)].reshape(total, HEAD_SIZE)

    dk, dv = head_gradients(
        q_ref[...], c_ref[...], head_of(0), head_of(KEY_VALUE_HEADS), bias,
        prob_ref, grad_ref, dq_ref,
    )
    dk_ref[...] = dk
    dv_ref[...] = dv

    for r in range(chips):

        @pl.when(step == r % KEY_VALUE_HEADS)
        def _():
            k = (chip + r) % chips
            for e in range(1, comp_count):
                from_column(k, e).wait_recv()
                pass_on(k, e, core).start()

    @pl.when(step == KEY_VALUE_HEADS - 1)
    def _():
        for t in range(chips - 1):

            @pl.when((chip - t >= 0) & (chip + 1 < chips))
            def _():
                up(t).wait_send()

            @pl.when((chip + t < chips) & (chip >= 1))
            def _():
                down(t).wait_send()

        for k in range(chips):
            to_sibling(k, core).wait_send()
            for e in range(1, comp_count):
                to_column(k, e).wait_send()
                pass_on(k, e, core).wait_send()
                pass_on(k, e, 1 - core).wait_recv()
        keep.wait()


def completion_kernel(
    ctx_count, comp_count, length_ref, chooser_ref, q_ref, c_ref, k_ref, v_ref, own_k_ref, own_v_ref,
    dq_ref, own_dk_ref, own_dv_ref, sum_ref,
    prob_ref, grad_ref, terms, arrived, table, table_in,
    send, recv, side_send, side_recv,
):
    step = pl.program_id(0)
    place = lax.axis_index("ctx")
    column = lax.axis_index("comp")
    rows = q_ref.shape[0]
    total = k_ref.shape[0]
    part = total // ctx_count
    length = length_ref[0]

    def other(offset):
        return (column + offset) % comp_count

    def out_to(h, d):
        target = (place + d) % ctx_count
        return remote(
            terms.at[h, target], arrived.at[h, d - 1], send.at[h, d - 1], recv.at[h, d - 1],
            target, column,
        )

    def across(h, e):
        return remote(
            table.at[h, e - 1], table_in.at[h, e - 1], side_send.at[h, e - 1],
            side_recv.at[h, e - 1], place, other(e),
        )

    @pl.when(step == 0)
    def _():
        greet(
            [((place + d) % ctx_count, column) for d in range(1, ctx_count)]
            + [(place, other(e)) for e in range(1, comp_count)]
        )

    key_at = lax.broadcasted_iota(jnp.int32, (rows, rows), 0)
    row_at = lax.broadcasted_iota(jnp.int32, (rows, rows), 1)
    own_bias = jnp.where((key_at <= row_at) & (key_at < length), 0.0, MASK_FILL)

    def bias(scores):
        own = scores[total:] + jnp.concatenate([own_bias] * PAIR, axis=1)
        return jnp.concatenate([scores[:total], own], axis=0)

    cotangent = c_ref[...]
    live = lax.broadcasted_iota(jnp.int32, cotangent.shape, 0) < length
    cotangent = jnp.where(live, cotangent, jnp.zeros_like(cotangent))
    keys = jnp.concatenate([k_ref[...], own_k_ref[...]], axis=0)
    values = jnp.concatenate([v_ref[...], own_v_ref[...]], axis=0)
    dk, dv = head_gradients(q_ref[...], cotangent, keys, values, bias, prob_ref, grad_ref, dq_ref)
    terms[step, :, :, :HEAD_SIZE] = dk[:total].reshape(ctx_count, part, HEAD_SIZE)
    terms[step, :, :, HEAD_SIZE:] = dv[:total].reshape(ctx_count, part, HEAD_SIZE)
    for d in range(1, ctx_count):
        out_to(step, d).start()
    own_dk_ref[...] = dk[total:]
    own_dv_ref[...] = dv[total:]

    @pl.when(step == KEY_VALUE_HEADS - 1)
    def _():
        def reduce_head(h, carry):
            for d in range(1, ctx_count):
                out_to(h, d).wait_recv()
            for e in list(range(1, comp_count)) + [0]:
                summed = terms[h, place].astype(jnp.float32) * chooser_ref[place, other(e)]
                for d in range(1, ctx_count):
                    source = (place + ctx_count - d) % ctx_count
                    weight = chooser_ref[source, other(e)]
                    summed += arrived[h, d - 1].astype(jnp.float32) * weight
                if e:
                    table[h, e - 1] = summed.astype(jnp.bfloat16)
                    across(h, e).start()
                else:
                    sum_ref[h] = summed
            return carry

        def finish_head(h, carry):
            summed = sum_ref[h]
            for e in range(1, comp_count):
                across(h, e).wait_recv()
                summed += table_in[h, e - 1].astype(jnp.float32)
            sum_ref[h] = summed
            for e in range(1, comp_count):
                across(h, e).wait_send()
            for d in range(1, ctx_count):
                out_to(h, d).wait_send()
            return carry

        lax.fori_loop(0, KEY_VALUE_HEADS, reduce_head, 0)
        lax.fori_loop(0, KEY_VALUE_HEADS, finish_head, 0)


def lane_block(rows, width, shift=0):
    return pl.BlockSpec((rows, width), lambda h: (0, h + shift))


def params(collective_id):
    return pltpu.CompilerParams(
        vmem_limit_bytes=56 * 1024 * 1024, collective_id=collective_id, has_side_effects=True
    )


def prompt_attention(query, cotangent, kv):
    ctx_count, comp_count = lax.axis_size("ctx"), lax.axis_size("comp")
    rows = query.shape[0]
    total = rows * ctx_count
    chips = ctx_count // 2
    wide = GROUP * HEAD_SIZE
    dma = pltpu.SemaphoreType.DMA
    return pl.pallas_call(
        functools.partial(prompt_kernel, ctx_count, comp_count),
        grid=(KEY_VALUE_HEADS,),
        in_specs=[
            lane_block(rows, wide),
            lane_block(rows, wide),
            pl.BlockSpec(kv.shape, lambda h: (0, 0)),
        ],
        out_specs=[
            lane_block(rows, wide),
            lane_block(total, HEAD_SIZE),
            lane_block(total, HEAD_SIZE),
            pl.BlockSpec(memory_space=pl.ANY),
        ],
        scratch_shapes=[
            pltpu.VMEM((ctx_count, rows, 2 * HALF), jnp.bfloat16),
            pltpu.VMEM((total, rows), jnp.float32),
            pltpu.VMEM((total, GROUP * rows), jnp.bfloat16),
            pltpu.VMEM((total, GROUP * rows), jnp.bfloat16),
        ]
        + [dma((chips - 1,))] * 4
        + [dma((chips,))] * 2
        + [dma((comp_count - 1, chips))] * 4
        + [dma],
        out_shape=[
            jax.ShapeDtypeStruct(query.shape, jnp.bfloat16),
            jax.ShapeDtypeStruct((total, HALF), jnp.bfloat16),
            jax.ShapeDtypeStruct((total, HALF), jnp.bfloat16),
            jax.ShapeDtypeStruct((comp_count, ctx_count, rows, 2 * HALF), jnp.bfloat16),
        ],
        compiler_params=params(1),
        name="prompt_attention",
    )(query, cotangent, kv)


def completion_attention(query, cotangent, kv, own_kv, length, chooser):
    ctx_count, comp_count = lax.axis_size("ctx"), lax.axis_size("comp")
    rows, total = query.shape[0], kv.shape[0]
    part = total // ctx_count
    wide = GROUP * HEAD_SIZE
    dma = pltpu.SemaphoreType.DMA
    sums = (KEY_VALUE_HEADS, part, 2 * HEAD_SIZE)
    return pl.pallas_call(
        functools.partial(completion_kernel, ctx_count, comp_count),
        grid=(KEY_VALUE_HEADS,),
        in_specs=[
            pl.BlockSpec(memory_space=pltpu.SMEM),
            pl.BlockSpec(memory_space=pltpu.SMEM),
            lane_block(rows, wide),
            lane_block(rows, wide),
            lane_block(total, HEAD_SIZE),
            lane_block(total, HEAD_SIZE, KEY_VALUE_HEADS),
            lane_block(rows, HEAD_SIZE),
            lane_block(rows, HEAD_SIZE, KEY_VALUE_HEADS),
        ],
        out_specs=[
            lane_block(rows, wide),
            lane_block(rows, HEAD_SIZE),
            lane_block(rows, HEAD_SIZE),
            pl.BlockSpec(sums, lambda h: (0, 0, 0)),
        ],
        scratch_shapes=[
            pltpu.VMEM((total + rows, GROUP * rows), jnp.bfloat16),
            pltpu.VMEM((total + rows, GROUP * rows), jnp.bfloat16),
            pltpu.VMEM((KEY_VALUE_HEADS, ctx_count, part, 2 * HEAD_SIZE), jnp.bfloat16),
            pltpu.VMEM((KEY_VALUE_HEADS, ctx_count - 1, part, 2 * HEAD_SIZE), jnp.bfloat16),
            pltpu.VMEM((KEY_VALUE_HEADS, comp_count - 1, part, 2 * HEAD_SIZE), jnp.bfloat16),
            pltpu.VMEM((KEY_VALUE_HEADS, comp_count - 1, part, 2 * HEAD_SIZE), jnp.bfloat16),
            dma((KEY_VALUE_HEADS, ctx_count - 1)),
            dma((KEY_VALUE_HEADS, ctx_count - 1)),
            dma((KEY_VALUE_HEADS, comp_count - 1)),
            dma((KEY_VALUE_HEADS, comp_count - 1)),
        ],
        out_shape=[
            jax.ShapeDtypeStruct(query.shape, jnp.bfloat16),
            jax.ShapeDtypeStruct((rows, HALF), jnp.bfloat16),
            jax.ShapeDtypeStruct((rows, HALF), jnp.bfloat16),
            jax.ShapeDtypeStruct(sums, jnp.float32),
        ],
        compiler_params=params(2),
        name="completion_attention",
    )(length, chooser, query, cotangent, kv, kv, own_kv, own_kv)


def local(prompt_query, prompt_kv, prompt_cot, comp_query, comp_kv, comp_cot, group_of, lengths):
    ctx_count = lax.axis_size("ctx")
    comp_count = lax.axis_size("comp")
    ctx_place = lax.axis_index("ctx")
    comp_place = lax.axis_index("comp")
    column_groups = jnp.take(group_of.reshape(ctx_count, comp_count), comp_place, axis=1)
    chooser = column_groups[:, None] == jnp.arange(comp_count, dtype=jnp.int32)[None, :]
    length = lax.dynamic_slice_in_dim(lengths, ctx_place * comp_count + comp_place, 1)
    prompt_dq, prompt_dk, prompt_dv, prompts = prompt_attention(
        prompt_query[0], prompt_cot[0], prompt_kv[0]
    )
    group_prompt = lax.dynamic_index_in_dim(prompts, column_groups[ctx_place], 0, keepdims=False)
    prompt_terms = jnp.concatenate([prompt_dk, prompt_dv], axis=1)
    own_terms = lax.psum_scatter(prompt_terms, "ctx", scatter_dimension=0, tiled=True)
    comp_dq, own_dk, own_dv, sums = completion_attention(
        comp_query[0],
        comp_cot[0],
        group_prompt.reshape(-1, 2 * HALF),
        comp_kv[0],
        length,
        chooser.astype(jnp.float32),
    )
    sums = jnp.concatenate(
        [sums[h, :, :HEAD_SIZE] for h in range(KEY_VALUE_HEADS)]
        + [sums[h, :, HEAD_SIZE:] for h in range(KEY_VALUE_HEADS)],
        axis=1,
    )
    summed = sums + own_terms.astype(jnp.float32)
    return (
        prompt_dq[None],
        summed.astype(jnp.bfloat16)[None],
        comp_dq[None],
        jnp.concatenate([own_dk, own_dv], axis=1)[None],
    )


def solution(mesh):
    placed = (
        P("comp", "ctx", None),
        P("comp", "ctx", None),
        P("comp", "ctx", None),
        P(("ctx", "comp"), None, None),
        P(("ctx", "comp"), None, None),
        P(("ctx", "comp"), None, None),
        P(),
        P(),
    )
    return jax.shard_map(
        local,
        mesh=mesh,
        in_specs=placed,
        out_specs=(
            P("comp", "ctx", None),
            P("comp", "ctx", None),
            P(("ctx", "comp"), None, None),
            P(("ctx", "comp"), None, None),
        ),
        check_vma=False,
    )
```

time: 236 us -> 176 us (0.75)
  waiting for transfers between devices: 96.2 us -> 0.02 us
  Pallas kernels: 46.8 us -> 138 us
  blocking collectives: 54.8 us -> 0 us
  local copies, waits for them, and re-layouts: 6.46 us -> 13.7 us
  starting transfers between devices: 5.58 us -> 0.04 us
    pallas_call x2, Pallas kernels: 46.8 us -> 138 us  [the longest x1 78.8 us: completion_attention(): pl.pallas_call(functools.partial(completion_kernel, ctx_count, comp_count...]
    all_gather x2 -> x0, waiting for transfers between devices: 67 us -> none  [the longest x1 39 us: local(): whole_prompt = lax.all_gather(prompt_kv[0], 'ctx', axis=0, tiled=True)]
    all_to_all x1 -> x0, blocking collectives: 54.8 us -> none  [local(): lax.all_to_all(outgoing_terms, 'ctx', split_axis=0, concat_axis=0, tiled=...]
    unnamed x5 -> x1, waiting for transfers between devices: 29.2 us -> 0.02 us
    unnamed x8 -> x17, local copies, waits for them, and re-layouts: 1.9 us -> 8.58 us
    all_to_all x1 -> x0, starting transfers between devices: 5.46 us -> none  [local(): lax.all_to_all(outgoing, 'ctx', split_axis=0, concat_axis=0, tiled=True)]
    dynamic_slice x0 -> x2, local copies, waits for them, and re-layouts: none -> 3.59 us  [the longest x1 3.07 us: local(): lax.dynamic_index_in_dim(prompts, column_groups[ctx_place], 0, keepdims=F...]
  transfers between devices with their start and end apart: 5 -> 1, of which waited for: 3 -> 0; matrix products, arithmetic and copies ran while one was open for 6% -> 8% of each run, Pallas kernels for 20% -> 45%
where the time goes in v1:
time: 176 us
  Pallas kernels  138 us (78%)
  between operations  16 us (9%)
  local copies, waits for them, and re-layouts  13.7 us (8%)
  other arithmetic  7.5 us (4%)
    pallas_call x1, Pallas kernels, completion_attention(): pl.pallas_call(functools.partial(completion_kernel, ctx_count, comp_count...  78.8 us
    pallas_call x1, Pallas kernels, prompt_attention(): pl.pallas_call(functools.partial(prompt_kernel, ctx_count, comp_count), g...  59.4 us
    unnamed x17, local copies, waits for them, and re-layouts  8.58 us
  transfers between devices with their start and end apart: 1, of which 0 were waited for; matrix products, arithmetic and copies ran while one was open for 8% of the time, Pallas kernels for 45%

profile of v1, /device:TPU:9, one launch (start us, length us, event | category | flops | bytes accessed | tf_op | source)
XLA Modules:
  0.0 175.5 jit_solution(4964706415830767615)
XLA Ops:
  7.2 0.0 reduce-scatter.2.cloned.1.call-start
  7.2 59.4 %prompt_attention.1 = (bf16[128,4096]{1,0:T(8,128)(2,1)}, bf16[1024,512]{1,0:T(8,128)(2,1)}, bf16[1024,512]{1,0:T(8,128)(2,1)}, bf16[4,8,128,1024]{3,2,1,0:T(8,128)(2,1)}) custom-call(bf16[128,4096]{1,0:T(8,128)(2,1)} %bitcast.36, bf16[128,4096]{1,0:T(8,128)(2,1)} %bitcast.37, bf16[128,1024]{1,0:T(8,128)(2,1)} %bitcast.40), custom_call_target="tpu_custom_call" | custom-call | tf_op jit(solution)/shard_map/prompt_attention/pallas_call | solution.py:364
  66.6 3.2 %pad_maximum_fusion = bf16[1024,1024]{1,0:T(8,128)(2,1)} fusion(bf16[1024,512]{1,0:T(8,128)(2,1)} %get-tuple-element.16, bf16[1024,512]{1,0:T(8,128)(2,1)} %get-tuple-element.15), kind=kLoop, calls=%fused_computation | loop fusion | flops 4194304 | bytes 4194304 | tf_op jit(solution)/shard_map/concatenate | solution.py:460
  69.8 0.0 copy-start.2
  69.8 0.0 copy-start.3
  69.8 0.0 reduce-scatter.2.cloned.1.call-update
  69.8 0.6 copy-done.2
  70.5 0.1 reshape.19
  70.5 0.2 fusion.2
  70.7 0.5 constant_dynamic-slice_fusion
  73.2 0.0 copy-done.3
  73.2 0.6 dynamic_slice.10.length_ref
  73.8 3.1 %constant_dynamic-slice_fusion.1 = bf16[1,8,128,1024]{3,2,1,0:T(8,128)(2,1)} fusion(bf16[4,8,128,1024]{3,2,1,0:T(8,128)(2,1)} %get-tuple-element.13, s32[]{:T(128)S(6)} %select_n.27), kind=kLoop, calls=%fused_computation.16 | loop fusion | bytes 4194308 | tf_op jit(solution)/shard_map/jit(dynamic_index_in_dim)/dynamic_slice | solution.py:459
  76.9 0.7 fusion.1.chooser_ref
  77.5 78.8 %completion_attention.1 = (bf16[128,4096]{1,0:T(8,128)(2,1)}, bf16[128,512]{1,0:T(8,128)(2,1)}, bf16[128,512]{1,0:T(8,128)(2,1)}, f32[4,128,256]{2,1,0:T(8,128)}) custom-call(s32[1]{0:T(128)} %dynamic_slice.10.length_ref, f32[8,4]{1,0:T(8,128)} %fusion.1.chooser_ref, bf16[128,4096]{1,0:T(8,128)(2,1)} %bitcast.32, bf16[128,4096]{1,0:T(8,128)(2,1)} %bitcast.33, ...), custom_call_target="tpu_custom_call" | custom-call | tf_op jit(solution)/shard_map/completion_attention/pallas_call | solution.py:406
  156.4 0.0 copy-start
  156.4 1.8 %maximum_bitcast_fusion = bf16[1,128,1024]{2,1,0:T(8,128)(2,1)} fusion(bf16[128,512]{1,0:T(8,128)(2,1)} %get-tuple-element.19, bf16[128,512]{1,0:T(8,128)(2,1)} %get-tuple-element.18), kind=kLoop, calls=%fused_computation.3 | loop fusion | flops 524288 | bytes 524288 | tf_op jit(solution)/shard_map/broadcast_in_dim | solution.py:480
  158.1 0.0 copy-start.1
  158.1 0.9 bitcast_dynamic-update-slice_fusion.7
  159.1 0.8 bitcast_dynamic-update-slice_fusion.6
  159.9 0.8 bitcast_dynamic-update-slice_fusion.5
  160.8 0.8 bitcast_dynamic-update-slice_fusion.4
  161.6 0.8 bitcast_dynamic-update-slice_fusion.3
  162.5 0.8 bitcast_dynamic-update-slice_fusion.2
  163.3 0.8 bitcast_dynamic-update-slice_fusion.1
  164.2 0.8 bitcast_dynamic-update-slice_fusion
  165.0 0.0 reduce-scatter.2.cloned.1.call-done
  165.0 1.7 fusion
  166.7 0.0 copy-done
  166.7 1.0 copy.21
  167.7 0.0 copy-done.1
  167.7 1.0 copy.22
Async XLA Ops:
  7.2 157.8 %reduce-scatter.2.cloned.1.call-start = ((), (), s32[]{:S(2)}) async-start(), calls=%async_computation.1 | async-start | bytes 2359296 | tf_op jit(solution)/shard_map/reduce_scatter | solution.py:461
  69.8 0.7 copy-start.2
  69.8 3.4 %copy-start.3 = (s32[32]{0:T(128)S(1)}, s32[32]{0:T(128)}, u32[]{:S(2)}) copy-start(s32[32]{0:T(128)} %param.15) | copy-start | bytes 388
  156.4 10.4 %copy-start = (bf16[128,4096]{1,0:T(8,128)(2,1)S(1)}, bf16[128,4096]{1,0:T(8,128)(2,1)}, u32[]{:S(2)}) copy-start(bf16[128,4096]{1,0:T(8,128)(2,1)} %get-tuple-element.12) | copy-start | bytes 3145732
  158.1 9.6 %copy-start.1 = (bf16[128,4096]{1,0:T(8,128)(2,1)S(1)}, bf16[128,4096]{1,0:T(8,128)(2,1)}, u32[]{:S(2)}) copy-start(bf16[128,4096]{1,0:T(8,128)(2,1)} %get-tuple-element.17) | copy-start | bytes 3145732
Sparse Core Ops, SparseCore 0:
  70.0 68.8 reduce-scatter.1

commit v2 on v1

--- a/solution.py
+++ b/solution.py
@@ -82,11 +82,19 @@
     pl.semaphore_wait(barrier, len(devices))
 
 
+def lanes_of(head):
+    return [
+        pl.ds(pl.multiple_of((head + shift) * HEAD_SIZE, HEAD_SIZE), HEAD_SIZE)
+        for shift in (0, KEY_VALUE_HEADS)
+    ]
+
+
 def prompt_kernel(
-    ctx_count, comp_count, q_ref, c_ref, kv_ref, dq_ref, dk_ref, dv_ref, all_ref,
-    whole, bias_ref, prob_ref, grad_ref,
+    ctx_count, comp_count, q_ref, c_ref, kv_ref, dq_ref, own_ref, all_ref,
+    whole, bias_ref, prob_ref, grad_ref, terms, pair_in, chip_terms, chip_in,
     up_send, up_recv, down_send, down_recv, pair_send, pair_recv,
     side_send, side_recv, pass_send, pass_recv, keep_sem,
+    half_send, half_recv, term_send, term_recv,
 ):
     step = pl.program_id(0)
     place = lax.axis_index("ctx")
@@ -161,6 +169,25 @@
             column,
         )
 
+    def half_over(h):
+        return remote(
+            terms.at[h, 1 - core], pair_in.at[h], half_send.at[h], half_recv.at[h], sibling, column
+        )
+
+    def terms_to(h, d):
+        target = (chip + d) % chips
+        return remote(
+            chip_terms.at[h, target], chip_in.at[h, d - 1], term_send.at[h, d - 1],
+            term_recv.at[h, d - 1], target * 2 + core, column,
+        )
+
+    def send_chip_terms(h):
+        half_over(h).wait_recv()
+        summed = terms[h, core].astype(jnp.float32) + pair_in[h].astype(jnp.float32)
+        chip_terms[h] = summed.astype(jnp.bfloat16)
+        for d in range(1, chips):
+            terms_to(h, d).start()
+
     keep = pltpu.make_async_copy(whole, all_ref.at[column], keep_sem)
 
     def share(k):
@@ -173,10 +200,9 @@
         whole[place] = kv_ref[...]
         greetings = [(sibling, column)]
         greetings += [(place, other(e)) for e in range(1, comp_count)]
-        greet(greetings + [
-            ((place + 2) % ctx_count, column),
-            ((place + ctx_count - 2) % ctx_count, column),
-        ])
+        greet(
+            greetings + [((place + 2 * d) % ctx_count, column) for d in range(1, chips)]
+        )
         for t in range(chips - 1):
 
             @pl.when((chip - t >= 0) & (chip + 1 < chips))
@@ -219,8 +245,16 @@
         q_ref[...], c_ref[...], head_of(0), head_of(KEY_VALUE_HEADS), bias,
         prob_ref, grad_ref, dq_ref,
     )
-    dk_ref[...] = dk
-    dv_ref[...] = dv
+    dk = dk.reshape(chips, 2, rows, HEAD_SIZE)
+    dv = dv.reshape(chips, 2, rows, HEAD_SIZE)
+    for side in range(2):
+        terms[step, side, :, :, :HEAD_SIZE] = dk[:, side]
+        terms[step, side, :, :, HEAD_SIZE:] = dv[:, side]
+    half_over(step).start()
+
+    @pl.when(step >= 1)
+    def _():
+        send_chip_terms(step - 1)
 
     for r in range(chips):
 
@@ -233,6 +267,18 @@
 
     @pl.when(step == KEY_VALUE_HEADS - 1)
     def _():
+        send_chip_terms(KEY_VALUE_HEADS - 1)
+        for h in range(KEY_VALUE_HEADS):
+            half_over(h).wait_send()
+            summed = chip_terms[h, chip].astype(jnp.float32)
+            for d in range(1, chips):
+                terms_to(h, d).wait_recv()
+                summed += chip_in[h, d - 1].astype(jnp.float32)
+            own_ref[:, h * HEAD_SIZE : (h + 1) * HEAD_SIZE] = summed[:, :HEAD_SIZE]
+            own_ref[:, HALF + h * HEAD_SIZE : HALF + (h + 1) * HEAD_SIZE] = summed[:, HEAD_SIZE:]
+            for d in range(1, chips):
+                terms_to(h, d).wait_send()
+
         for t in range(chips - 1):
 
             @pl.when((chip - t >= 0) & (chip + 1 < chips))
@@ -254,8 +300,8 @@
 
 def completion_kernel(
     ctx_count, comp_count, length_ref, chooser_ref, q_ref, c_ref, k_ref, v_ref, own_k_ref, own_v_ref,
-    dq_ref, own_dk_ref, own_dv_ref, sum_ref,
-    prob_ref, grad_ref, terms, arrived, table, table_in,
+    prompt_ref, dq_ref, own_ref, out_ref,
+    sum_ref, prob_ref, grad_ref, terms, arrived, table, table_in,
     send, recv, side_send, side_recv,
 ):
     step = pl.program_id(0)
@@ -307,8 +353,9 @@
     terms[step, :, :, HEAD_SIZE:] = dv[:total].reshape(ctx_count, part, HEAD_SIZE)
     for d in range(1, ctx_count):
         out_to(step, d).start()
-    own_dk_ref[...] = dk[total:]
-    own_dv_ref[...] = dv[total:]
+    key_lanes, value_lanes = lanes_of(step)
+    own_ref[:, key_lanes] = dk[total:]
+    own_ref[:, value_lanes] = dv[total:]
 
     @pl.when(step == KEY_VALUE_HEADS - 1)
     def _():
@@ -333,7 +380,9 @@
             for e in range(1, comp_count):
                 across(h, e).wait_recv()
                 summed += table_in[h, e - 1].astype(jnp.float32)
-            sum_ref[h] = summed
+            for at, lanes in enumerate(lanes_of(h)):
+                part_sum = summed[:, at * HEAD_SIZE : (at + 1) * HEAD_SIZE]
+                out_ref[:, lanes] = (part_sum + prompt_ref[:, lanes]).astype(jnp.bfloat16)
             for e in range(1, comp_count):
                 across(h, e).wait_send()
             for d in range(1, ctx_count):
@@ -371,8 +420,7 @@
         ],
         out_specs=[
             lane_block(rows, wide),
-            lane_block(total, HEAD_SIZE),
-            lane_block(total, HEAD_SIZE),
+            pl.BlockSpec(kv.shape, lambda h: (0, 0)),
             pl.BlockSpec(memory_space=pl.ANY),
         ],
         scratch_shapes=[
@@ -380,15 +428,20 @@
             pltpu.VMEM((total, rows), jnp.float32),
             pltpu.VMEM((total, GROUP * rows), jnp.bfloat16),
             pltpu.VMEM((total, GROUP * rows), jnp.bfloat16),
+            pltpu.VMEM((KEY_VALUE_HEADS, 2, chips, rows, 2 * HEAD_SIZE), jnp.bfloat16),
+            pltpu.VMEM((KEY_VALUE_HEADS, chips, rows, 2 * HEAD_SIZE), jnp.bfloat16),
+            pltpu.VMEM((KEY_VALUE_HEADS, chips, rows, 2 * HEAD_SIZE), jnp.bfloat16),
+            pltpu.VMEM((KEY_VALUE_HEADS, chips - 1, rows, 2 * HEAD_SIZE), jnp.bfloat16),
         ]
         + [dma((chips - 1,))] * 4
         + [dma((chips,))] * 2
         + [dma((comp_count - 1, chips))] * 4
-        + [dma],
+        + [dma]
+        + [dma((KEY_VALUE_HEADS,))] * 2
+        + [dma((KEY_VALUE_HEADS, chips - 1))] * 2,
         out_shape=[
             jax.ShapeDtypeStruct(query.shape, jnp.bfloat16),
-            jax.ShapeDtypeStruct((total, HALF), jnp.bfloat16),
-            jax.ShapeDtypeStruct((total, HALF), jnp.bfloat16),
+            jax.ShapeDtypeStruct(kv.shape, jnp.float32),
             jax.ShapeDtypeStruct((comp_count, ctx_count, rows, 2 * HALF), jnp.bfloat16),
         ],
         compiler_params=params(1),
@@ -396,7 +449,7 @@
     )(query, cotangent, kv)
 
 
-def completion_attention(query, cotangent, kv, own_kv, length, chooser):
+def completion_attention(query, cotangent, kv, own_kv, prompt_sum, length, chooser):
     ctx_count, comp_count = lax.axis_size("ctx"), lax.axis_size("comp")
     rows, total = query.shape[0], kv.shape[0]
     part = total // ctx_count
@@ -415,14 +468,15 @@
             lane_block(total, HEAD_SIZE, KEY_VALUE_HEADS),
             lane_block(rows, HEAD_SIZE),
             lane_block(rows, HEAD_SIZE, KEY_VALUE_HEADS),
+            pl.BlockSpec(prompt_sum.shape, lambda h: (0, 0)),
         ],
         out_specs=[
             lane_block(rows, wide),
-            lane_block(rows, HEAD_SIZE),
-            lane_block(rows, HEAD_SIZE),
-            pl.BlockSpec(sums, lambda h: (0, 0, 0)),
+            pl.BlockSpec(own_kv.shape, lambda h: (0, 0)),
+            pl.BlockSpec(prompt_sum.shape, lambda h: (0, 0)),
         ],
         scratch_shapes=[
+            pltpu.VMEM(sums, jnp.float32),
             pltpu.VMEM((total + rows, GROUP * rows), jnp.bfloat16),
             pltpu.VMEM((total + rows, GROUP * rows), jnp.bfloat16),
             pltpu.VMEM((KEY_VALUE_HEADS, ctx_count, part, 2 * HEAD_SIZE), jnp.bfloat16),
@@ -436,13 +490,12 @@
         ],
         out_shape=[
             jax.ShapeDtypeStruct(query.shape, jnp.bfloat16),
-            jax.ShapeDtypeStruct((rows, HALF), jnp.bfloat16),
-            jax.ShapeDtypeStruct((rows, HALF), jnp.bfloat16),
-            jax.ShapeDtypeStruct(sums, jnp.float32),
+            jax.ShapeDtypeStruct(own_kv.shape, jnp.bfloat16),
+            jax.ShapeDtypeStruct(prompt_sum.shape, jnp.bfloat16),
         ],
         compiler_params=params(2),
         name="completion_attention",
-    )(length, chooser, query, cotangent, kv, kv, own_kv, own_kv)
+    )(length, chooser, query, cotangent, kv, kv, own_kv, own_kv, prompt_sum)
 
 
 def local(prompt_query, prompt_kv, prompt_cot, comp_query, comp_kv, comp_cot, group_of, lengths):
@@ -453,32 +506,20 @@
     column_groups = jnp.take(group_of.reshape(ctx_count, comp_count), comp_place, axis=1)
     chooser = column_groups[:, None] == jnp.arange(comp_count, dtype=jnp.int32)[None, :]
     length = lax.dynamic_slice_in_dim(lengths, ctx_place * comp_count + comp_place, 1)
-    prompt_dq, prompt_dk, prompt_dv, prompts = prompt_attention(
+    prompt_dq, prompt_sum, prompts = prompt_attention(
         prompt_query[0], prompt_cot[0], prompt_kv[0]
     )
     group_prompt = lax.dynamic_index_in_dim(prompts, column_groups[ctx_place], 0, keepdims=False)
-    prompt_terms = jnp.concatenate([prompt_dk, prompt_dv], axis=1)
-    own_terms = lax.psum_scatter(prompt_terms, "ctx", scatter_dimension=0, tiled=True)
-    comp_dq, own_dk, own_dv, sums = completion_attention(
+    comp_dq, own_dkv, summed = completion_attention(
         comp_query[0],
         comp_cot[0],
         group_prompt.reshape(-1, 2 * HALF),
         comp_kv[0],
+        prompt_sum,
         length,
         chooser.astype(jnp.float32),
     )
-    sums = jnp.concatenate(
-        [sums[h, :, :HEAD_SIZE] for h in range(KEY_VALUE_HEADS)]
-        + [sums[h, :, HEAD_SIZE:] for h in range(KEY_VALUE_HEADS)],
-        axis=1,
-    )
-    summed = sums + own_terms.astype(jnp.float32)
-    return (
-        prompt_dq[None],
-        summed.astype(jnp.bfloat16)[None],
-        comp_dq[None],
-        jnp.concatenate([own_dk, own_dv], axis=1)[None],
-    )
+    return prompt_dq[None], summed[None], comp_dq[None], own_dkv[None]
 
 
 def solution(mesh):

time: 176 us -> 152 us (0.86)
  between operations: 16 us -> 2.62 us
  other arithmetic: 7.5 us -> 0.85 us
  Pallas kernels: 138 us -> 136 us
    pallas_call x1, Pallas kernels: 78.8 us -> 65 us  [completion_attention(): pl.pallas_call(functools.partial(completion_kernel, ctx_count, comp_count...]
    pallas_call x1, Pallas kernels: 59.4 us -> 70.9 us  [prompt_attention(): pl.pallas_call(functools.partial(prompt_kernel, ctx_count, comp_count), g...]
    broadcast_in_dim x2 -> x0, other arithmetic: 3.49 us -> none  [the longest x1 1.78 us: local(): jnp.concatenate([own_dk, own_dv], axis=1)[None]]
    concatenate x1 -> x0, other arithmetic: 3.16 us -> none  [local(): prompt_terms = jnp.concatenate([prompt_dk, prompt_dv], axis=1)]
    unnamed x17 -> x6, local copies, waits for them, and re-layouts: 8.58 us -> 6.6 us
  transfers between devices with their start and end apart: 1 -> 0, of which waited for: 0 -> 0; matrix products, arithmetic and copies ran while one was open for 8% -> 0% of each run, Pallas kernels for 45% -> 0%
where the time goes in v2:
time: 152 us
  Pallas kernels  136 us (89%)
  local copies, waits for them, and re-layouts  12.3 us (8%)
  between operations  2.62 us (2%)
    pallas_call x1, Pallas kernels, prompt_attention(): pl.pallas_call(functools.partial(prompt_kernel, ctx_count, comp_count), g...  70.9 us
    pallas_call x1, Pallas kernels, completion_attention(): pl.pallas_call(functools.partial(completion_kernel, ctx_count, comp_count...  65 us
    unnamed x6, local copies, waits for them, and re-layouts  6.6 us
    dynamic_slice x1, local copies, waits for them, and re-layouts, local(): lax.dynamic_index_in_dim(prompts, column_groups[ctx_place], 0, keepdims=F...  3.23 us

profile of v2, /device:TPU:9, one launch (start us, length us, event | category | flops | bytes accessed | tf_op | source)
XLA Modules:
  0.0 151.8 jit_solution(14604498903968956699)
XLA Ops:
  0.6 0.7 reshape.19
  1.4 0.2 fusion.1
  1.6 0.5 constant_dynamic-slice_fusion
  4.0 70.9 %prompt_attention.1 = (bf16[128,4096]{1,0:T(8,128)(2,1)}, f32[128,1024]{1,0:T(8,128)}, bf16[4,8,128,1024]{3,2,1,0:T(8,128)(2,1)}) custom-call(bf16[128,4096]{1,0:T(8,128)(2,1)} %bitcast.18, bf16[128,4096]{1,0:T(8,128)(2,1)} %bitcast.19, bf16[128,1024]{1,0:T(8,128)(2,1)} %bitcast.22), custom_call_target="tpu_custom_call" | custom-call | tf_op jit(solution)/shard_map/prompt_attention/pallas_call | solution.py:413
  75.0 0.0 copy-start
  75.0 3.2 %constant_dynamic-slice_fusion.1 = bf16[1,8,128,1024]{3,2,1,0:T(8,128)(2,1)} fusion(bf16[4,8,128,1024]{3,2,1,0:T(8,128)(2,1)} %get-tuple-element.11, s32[]{:T(128)S(6)} %select_n.27), kind=kLoop, calls=%fused_computation.4 | loop fusion | bytes 4194308 | tf_op jit(solution)/shard_map/jit(dynamic_index_in_dim)/dynamic_slice | solution.py:512
  78.2 0.7 fusion.chooser_ref
  78.9 1.2 dynamic_slice.10.length_ref
  80.1 65.0 %completion_attention.1 = (bf16[128,4096]{1,0:T(8,128)(2,1)}, bf16[128,1024]{1,0:T(8,128)(2,1)}, bf16[128,1024]{1,0:T(8,128)(2,1)}) custom-call(s32[1]{0:T(128)} %dynamic_slice.10.length_ref, f32[8,4]{1,0:T(8,128)} %fusion.chooser_ref, bf16[128,4096]{1,0:T(8,128)(2,1)} %bitcast.14, bf16[128,4096]{1,0:T(8,128)(2,1)} %bitcast.15, bf16[1024,1024]{1,0:T(8,128)(2,1)} %bitcast.12, ...), custom_call_target="tpu_custom_call" | custom-call | tf_op jit(solution)/shard_map/completion_attention/pallas_call | solution.py:459
  145.2 0.0 copy-done
  145.2 1.0 copy.16
  146.1 1.7 %copy.17 = bf16[1,128,1024]{2,1,0:T(8,128)(2,1)} copy(bf16[1,128,1024]{2,1,0:T(8,128)(2,1)} %bitcast.24) | data formatting | bytes 524288
  147.8 2.3 %copy.18 = bf16[1,128,4096]{2,1,0:T(8,128)(2,1)} copy(bf16[1,128,4096]{2,1,0:T(8,128)(2,1)} %bitcast.21) | data formatting | bytes 2097152
  150.1 1.7 %copy.19 = bf16[1,128,1024]{2,1,0:T(8,128)(2,1)} copy(bf16[1,128,1024]{2,1,0:T(8,128)(2,1)} %bitcast.23) | data formatting | bytes 524288
Async XLA Ops:
  75.0 70.2 %copy-start = (bf16[128,4096]{1,0:T(8,128)(2,1)S(1)}, bf16[128,4096]{1,0:T(8,128)(2,1)}, u32[]{:S(2)}) copy-start(bf16[128,4096]{1,0:T(8,128)(2,1)} %get-tuple-element.10) | copy-start | bytes 3145732

commit v3 on v2

--- a/solution.py
+++ b/solution.py
@@ -258,7 +258,7 @@
 
     for r in range(chips):
 
-        @pl.when(step == r % KEY_VALUE_HEADS)
+        @pl.when(step == min(r % KEY_VALUE_HEADS + 1, KEY_VALUE_HEADS - 1))
         def _():
             k = (chip + r) % chips
             for e in range(1, comp_count):

time: 152 us -> 147 us (0.967)
  Pallas kernels: 136 us -> 131 us
    pallas_call x1, Pallas kernels: 70.9 us -> 65.5 us  [prompt_attention(): pl.pallas_call(functools.partial(prompt_kernel, ctx_count, comp_count), g...]
where the time goes in v3:
time: 147 us; the launch traced here: 146 us
  Pallas kernels  131 us (89%)
  local copies, waits for them, and re-layouts  12.3 us (8%)
  between operations  2.62 us (2%)
    pallas_call x1, Pallas kernels, prompt_attention(): pl.pallas_call(functools.partial(prompt_kernel, ctx_count, comp_count), g...  65.5 us
    pallas_call x1, Pallas kernels, completion_attention(): pl.pallas_call(functools.partial(completion_kernel, ctx_count, comp_count...  65.1 us
    unnamed x6, local copies, waits for them, and re-layouts  6.6 us
    dynamic_slice x1, local copies, waits for them, and re-layouts, local(): lax.dynamic_index_in_dim(prompts, column_groups[ctx_place], 0, keepdims=F...  3.23 us

profile of v3, /device:TPU:9, one launch (start us, length us, event | category | flops | bytes accessed | tf_op | source)
XLA Modules:
  0.0 146.4 jit_solution(11462898645099886469)
XLA Ops:
  0.6 0.7 reshape.19
  1.4 0.2 fusion.1
  1.6 0.5 constant_dynamic-slice_fusion
  4.0 65.5 %prompt_attention.1 = (bf16[128,4096]{1,0:T(8,128)(2,1)}, f32[128,1024]{1,0:T(8,128)}, bf16[4,8,128,1024]{3,2,1,0:T(8,128)(2,1)}) custom-call(bf16[128,4096]{1,0:T(8,128)(2,1)} %bitcast.18, bf16[128,4096]{1,0:T(8,128)(2,1)} %bitcast.19, bf16[128,1024]{1,0:T(8,128)(2,1)} %bitcast.22), custom_call_target="tpu_custom_call" | custom-call | tf_op jit(solution)/shard_map/prompt_attention/pallas_call | solution.py:413
  69.5 0.0 copy-start
  69.5 3.2 %constant_dynamic-slice_fusion.1 = bf16[1,8,128,1024]{3,2,1,0:T(8,128)(2,1)} fusion(bf16[4,8,128,1024]{3,2,1,0:T(8,128)(2,1)} %get-tuple-element.11, s32[]{:T(128)S(6)} %select_n.27), kind=kLoop, calls=%fused_computation.4 | loop fusion | bytes 4194308 | tf_op jit(solution)/shard_map/jit(dynamic_index_in_dim)/dynamic_slice | solution.py:512
  72.8 0.7 fusion.chooser_ref
  73.4 1.2 dynamic_slice.10.length_ref
  74.7 65.1 %completion_attention.1 = (bf16[128,4096]{1,0:T(8,128)(2,1)}, bf16[128,1024]{1,0:T(8,128)(2,1)}, bf16[128,1024]{1,0:T(8,128)(2,1)}) custom-call(s32[1]{0:T(128)} %dynamic_slice.10.length_ref, f32[8,4]{1,0:T(8,128)} %fusion.chooser_ref, bf16[128,4096]{1,0:T(8,128)(2,1)} %bitcast.14, bf16[128,4096]{1,0:T(8,128)(2,1)} %bitcast.15, bf16[1024,1024]{1,0:T(8,128)(2,1)} %bitcast.12, ...), custom_call_target="tpu_custom_call" | custom-call | tf_op jit(solution)/shard_map/completion_attention/pallas_call | solution.py:459
  139.8 0.0 copy-done
  139.8 1.0 copy.16
  140.8 1.7 %copy.17 = bf16[1,128,1024]{2,1,0:T(8,128)(2,1)} copy(bf16[1,128,1024]{2,1,0:T(8,128)(2,1)} %bitcast.24) | data formatting | bytes 524288
  142.4 2.3 %copy.18 = bf16[1,128,4096]{2,1,0:T(8,128)(2,1)} copy(bf16[1,128,4096]{2,1,0:T(8,128)(2,1)} %bitcast.21) | data formatting | bytes 2097152
  144.7 1.7 %copy.19 = bf16[1,128,1024]{2,1,0:T(8,128)(2,1)} copy(bf16[1,128,1024]{2,1,0:T(8,128)(2,1)} %bitcast.23) | data formatting | bytes 524288
Async XLA Ops:
  69.5 70.3 %copy-start = (bf16[128,4096]{1,0:T(8,128)(2,1)S(1)}, bf16[128,4096]{1,0:T(8,128)(2,1)}, u32[]{:S(2)}) copy-start(bf16[128,4096]{1,0:T(8,128)(2,1)} %get-tuple-element.10) | copy-start | bytes 3145732
